TPU v7x, 32 devices: a whole 2x2x4 slice. The times are simulated.
32 devices in a mesh: dp: 8 (over z, y), mp: 4 (over x, core).
Axes of the slice: x: 2, y: 2, z: 4, core: 2. Of those that a mesh axis runs over, the one named last changes fastest.
Arguments:
- features_in: bfloat16 [16, 24576], P(None, 'dp'), may hold values from -6 to 6
- w_in: bfloat16 [16, 1024], P(None, 'mp'), may hold values from -1.5 to 1.5
- w_mid: bfloat16 [1024, 1024], P(None, 'mp'), may hold values from -0.1875 to 0.1875
- w_out: bfloat16 [1024], P('mp'), may hold values from -0.1875 to 0.1875
- targets: float32 [24576], P('dp'), may hold values from -6 to 6
- valid_steps: int32 [256], P('dp'), may hold values from 16 to 96, as said below
Outputs:
- predicted_change: float32 [24576], P('dp')
Inputs may be any that keep to these rules, and one draw needn't show every extreme that they name: `valid_steps`: the last building has all 96 valid steps.
All inputs are finite; a program needn't handle non-finite values.
Results may differ from a plain program's by a relative error of at most 0.00037.
Values may be sent and summed in bfloat16 or wider, within the bound.
A program may use at most 64 MiB of HBM per device.

v0:
```python
import jax
import jax.numpy as jnp
from jax import lax
from jax.sharding import PartitionSpec as P

STEPS = 96
ITERS = 3
damping = 0.002


def pull_back(columns, back):
    return lax.dot_general(
        columns, back, (((0,), (0,)), ((), ())), preferred_element_type=jnp.float32
    )


def shards(features_in, w_in, w_mid, w_out, targets, valid_steps):
    out_weight = w_out.astype(jnp.float32)
    valid_count = lax.psum(jnp.sum(valid_steps).astype(jnp.float32), "dp")
    whole_input = lax.all_gather(w_in, "mp", axis=1, tiled=True)
    hidden_one = jnp.tanh(
        jnp.dot(features_in.T, whole_input, preferred_element_type=jnp.float32)
    ).astype(jnp.bfloat16)
    hidden_two = jnp.tanh(jnp.dot(hidden_one, w_mid, preferred_element_type=jnp.float32))
    slope_out = (1.0 - hidden_two * hidden_two) * out_weight
    predicted = lax.psum(jnp.sum(hidden_two * out_weight, axis=-1), "mp")
    step_mask = (
        (jnp.arange(STEPS, dtype=jnp.int32)[None, :] < valid_steps[:, None])
        .astype(jnp.float32)
        .reshape(-1)
    )
    row_weight = step_mask / valid_count
    error_rows = row_weight * (predicted - targets)
    grad_back = (error_rows[:, None] * slope_out).astype(jnp.bfloat16)

    def tangent(dir_bf16):
        partial_rows = jnp.sum(
            jnp.dot(hidden_one, dir_bf16, preferred_element_type=jnp.float32) * slope_out, axis=-1
        )
        return lax.psum(partial_rows, "mp")

    gradient = lax.psum(pull_back(hidden_one, grad_back), "dp")

    def spread(vector):
        return vector.astype(jnp.bfloat16)

    def inner_product(first, second):
        return lax.psum(jnp.sum(first * second), "mp")

    solution = jnp.zeros_like(gradient)
    remainder = -gradient
    direction = remainder
    norm_now = inner_product(remainder, remainder)
    for iteration in range(ITERS):
        summed = lax.psum(
            pull_back(
                hidden_one,
                ((row_weight * tangent(spread(direction)))[:, None] * slope_out).astype(
                    jnp.bfloat16
                ),
            ),
            "dp",
        )
        curved = summed + damping * direction
        step_size = norm_now / inner_product(direction, curved)
        solution = solution + step_size * direction
        remainder = remainder - step_size * curved
        if iteration + 1 < ITERS:
            norm_next = inner_product(remainder, remainder)
            direction = remainder + norm_next / norm_now * direction
            norm_now = norm_next
    return tangent(spread(solution))


def solution(mesh):
    return jax.shard_map(
        shards,
        mesh=mesh,
        in_specs=(P(None, "dp"), P(None, "mp"), P(None, "mp"), P("mp"), P("dp"), P("dp")),
        out_specs=P("dp"),
        check_vma=False,
    )
```

profile of v0, /device:TPU:0, one launch (start us, length us, event | category | flops | bytes accessed | tf_op | source)
XLA Modules:
  0.0 518.2 jit_solution(10270129785186823184)
XLA Ops:
  8.5 23.6 %psum.112 = f32[]{:T(128)} all-reduce(f32[]{:T(128)S(6)} %convert_element_type.36), channel_id=1, replica_groups=mesh['dp'=8,'mp'=4] {'dp'}, use_global_device_ids=true, to_apply=%region_1.0 | all-reduce | flops 1 | bytes 8 | tf_op jit(solution)/shard_map/psum | solution.py:19
  34.3 5.4 %all_gather.3 = bf16[16,1024]{1,0:T(8,128)(2,1)S(1)} all-gather(bf16[16,256]{1,0:T(8,128)(2,1)} %param.7), channel_id=1, replica_groups=mesh['dp'=8,'mp'=4] {'mp'}, dimensions={1}, use_global_device_ids=true | all-gather | bytes 40960 | tf_op jit(solution)/shard_map/all_gather | solution.py:20
  46.3 11.3 %psum.113 = f32[3072]{0:T(1024)S(1)} all-reduce(f32[3072]{0:T(1024)S(1)} %get-tuple-element.11), channel_id=1, replica_groups=mesh['dp'=8,'mp'=4] {'mp'}, use_global_device_ids=true, to_apply=%region_3.0 | all-reduce | flops 3072 | bytes 24576 | tf_op jit(solution)/shard_map/psum | solution.py:26
  57.6 6.7 %fusion = f32[1024,256]{1,0:T(8,128)} fusion(bf16[3072,1024]{1,0:T(8,128)(2,1)} %copy-done.1, f32[3072]{0:T(1024)S(1)} %subtract_multiply_fusion.1, f32[3072,256]{0,1:T(8,128)} %get-tuple-element.12, f32[256]{0:T(256)S(1)} %convert_element_type.37), kind=kOutput, calls=%fused_computation.12 | convolution fusion | flops 1614544896 | bytes 10499072 | tf_op jit(solution)/shard_map/dot_general | solution.py:12
  64.4 74.4 %all-reduce.6.cloned.1.call-done = f32[1024,256]{1,0:T(8,128)} async-done(((f32[1024,256]{1,0:T(8,128)}), f32[1024,256]{1,0:T(8,128)}) %all-reduce.6.cloned.1.call-update) | async-done | bytes 1048592 | tf_op jit(solution)/shard_map/psum | solution.py:42
  138.8 6.2 %fusion.8 = f32[3072]{0:T(1024)S(1)} fusion(bf16[3072,1024]{1,0:T(8,128)(2,1)} %copy-done.1, f32[1024,256]{1,0:T(8,128)} %all-reduce.6.cloned.1.call-done, f32[256]{0:T(256)S(1)} %convert_element_type.37, f32[3072,256]{0,1:T(8,128)} %get-tuple-element.12), kind=kOutput, calls=%fused_computation.20 | convolution fusion | flops 1615066112 | bytes 10499072 | tf_op jit(solution)/shard_map/dot_general | solution.py:38
  145.0 10.2 %psum.116 = f32[3072]{0:T(1024)S(1)} all-reduce(f32[3072]{0:T(1024)S(1)} %fusion.8), channel_id=1, replica_groups=mesh['dp'=8,'mp'=4] {'mp'}, use_global_device_ids=true, to_apply=%region_8.0 | all-reduce | flops 3072 | bytes 24576 | tf_op jit(solution)/shard_map/psum | solution.py:40
  155.2 6.8 %fusion.1 = f32[1024,256]{1,0:T(8,128)} fusion(bf16[3072,1024]{1,0:T(8,128)(2,1)} %copy-done.1, f32[3072]{0:T(1024)S(1)} %mul.147, f32[3072,256]{0,1:T(8,128)} %get-tuple-element.12, f32[256]{0:T(256)S(1)} %convert_element_type.37), kind=kOutput, calls=%fused_computation.13 | convolution fusion | flops 1614544896 | bytes 10499072 | tf_op jit(solution)/shard_map/dot_general | solution.py:12
  162.2 77.6 %all-reduce.8.cloned.1.call-done = f32[1024,256]{1,0:T(8,128)} async-done(((f32[1024,256]{1,0:T(8,128)}), f32[1024,256]{1,0:T(8,128)}) %all-reduce.8.cloned.1.call-update) | async-done | bytes 1048592 | tf_op jit(solution)/shard_map/psum | solution.py:55
  242.0 6.5 %all-reduce = (f32[]{:T(128)}, f32[]{:T(128)}) all-reduce(f32[]{:T(128)} %get-tuple-element.6, f32[]{:T(128)} %get-tuple-element.5), channel_id=1, replica_groups=mesh['dp'=8,'mp'=4] {'mp'}, use_global_device_ids=true, to_apply=%region_6.0 | all-reduce | flops 2 | bytes 16 | tf_op jit(solution)/shard_map/psum | solution.py:48
  251.9 7.0 %psum.119 = f32[]{:T(128)} all-reduce(f32[]{:T(128)} %get-tuple-element.9), channel_id=1, replica_groups=mesh['dp'=8,'mp'=4] {'mp'}, use_global_device_ids=true, to_apply=%region_13.0 | all-reduce | flops 1 | bytes 8 | tf_op jit(solution)/shard_map/psum | solution.py:48
  262.4 5.1 fusion.9
  267.6 10.2 %psum.120 = f32[3072]{0:T(1024)S(1)} all-reduce(f32[3072]{0:T(1024)S(1)} %fusion.9), channel_id=1, replica_groups=mesh['dp'=8,'mp'=4] {'mp'}, use_global_device_ids=true, to_apply=%region_15.0 | all-reduce | flops 3072 | bytes 24576 | tf_op jit(solution)/shard_map/psum | solution.py:40
  277.8 6.7 %fusion.2 = f32[1024,256]{1,0:T(8,128)} fusion(bf16[3072,1024]{1,0:T(8,128)(2,1)} %copy-done.1, f32[3072]{0:T(1024)S(1)} %mul.159, f32[3072,256]{0,1:T(8,128)} %get-tuple-element.12, f32[256]{0:T(256)S(1)} %convert_element_type.37), kind=kOutput, calls=%fused_computation.14 | convolution fusion | flops 1614544896 | bytes 10499072 | tf_op jit(solution)/shard_map/dot_general | solution.py:12
  284.6 77.0 %all-reduce.10.cloned.1.call-done = f32[1024,256]{1,0:T(8,128)} async-done(((f32[1024,256]{1,0:T(8,128)}), f32[1024,256]{1,0:T(8,128)}) %all-reduce.10.cloned.1.call-update) | async-done | bytes 1048592 | tf_op jit(solution)/shard_map/psum | solution.py:55
  363.7 6.5 %psum.122 = f32[]{:T(128)} all-reduce(f32[]{:T(128)} %multiply_reduce_fusion.3), channel_id=1, replica_groups=mesh['dp'=8,'mp'=4] {'mp'}, use_global_device_ids=true, to_apply=%region_18.0 | all-reduce | flops 1 | bytes 8 | tf_op jit(solution)/shard_map/psum | solution.py:48
  373.6 7.0 %psum.123 = f32[]{:T(128)} all-reduce(f32[]{:T(128)} %multiply_reduce_fusion.2), channel_id=1, replica_groups=mesh['dp'=8,'mp'=4] {'mp'}, use_global_device_ids=true, to_apply=%region_20.0 | all-reduce | flops 1 | bytes 8 | tf_op jit(solution)/shard_map/psum | solution.py:48
  384.5 5.2 fusion.10
  389.6 10.2 %psum.124 = f32[3072]{0:T(1024)S(1)} all-reduce(f32[3072]{0:T(1024)S(1)} %fusion.10), channel_id=1, replica_groups=mesh['dp'=8,'mp'=4] {'mp'}, use_global_device_ids=true, to_apply=%region_22.0 | all-reduce | flops 3072 | bytes 24576 | tf_op jit(solution)/shard_map/psum | solution.py:40
  399.8 6.8 %fusion.3 = f32[1024,256]{1,0:T(8,128)} fusion(bf16[3072,1024]{1,0:T(8,128)(2,1)} %copy-done.1, f32[3072]{0:T(1024)S(1)} %mul.171, f32[3072,256]{0,1:T(8,128)} %get-tuple-element.12, f32[256]{0:T(256)S(1)} %convert_element_type.37), kind=kOutput, calls=%fused_computation.15 | convolution fusion | flops 1614544896 | bytes 10499072 | tf_op jit(solution)/shard_map/dot_general | solution.py:12
  406.7 77.1 %all-reduce.12.cloned.1.call-done = f32[1024,256]{1,0:T(8,128)} async-done(((f32[1024,256]{1,0:T(8,128)}), f32[1024,256]{1,0:T(8,128)}) %all-reduce.12.cloned.1.call-update) | async-done | bytes 1048592 | tf_op jit(solution)/shard_map/psum | solution.py:55
  486.2 6.7 %psum.126 = f32[]{:T(128)} all-reduce(f32[]{:T(128)} %multiply_reduce_fusion.1), channel_id=1, replica_groups=mesh['dp'=8,'mp'=4] {'mp'}, use_global_device_ids=true, to_apply=%region_25.0 | all-reduce | flops 1 | bytes 8 | tf_op jit(solution)/shard_map/psum | solution.py:48
  494.1 6.3 %fusion.11 = f32[3072]{0:T(1024)S(1)} fusion(bf16[3072,1024]{1,0:T(8,128)(2,1)} %copy-done.1, f32[1024,256]{1,0:T(8,128)} %copy-done.4, f32[1024,256]{1,0:T(8,128)S(1)} %multiply_add_fusion.2, f32[1024,256]{1,0:T(8,128)S(1)} %copy-done.3, f32[]{:T(128)S(6)} %div.30, f32[]{:T(128)S(6)} %div.28, f32[]{:T(128)S(6)} %div.26, f32[256]{0:T(256)S(1)} %convert_element_type.37, ...), kind=kOutput, calls=%fused_computation.23 | convolution fusion | flops 1616376832 | bytes 12596236 | tf_op jit(solution)/shard_map/dot_general | solution.py:38
  500.4 11.2 %psum.127 = f32[3072]{0:T(1024)} all-reduce(f32[3072]{0:T(1024)S(1)} %fusion.11), channel_id=1, replica_groups=mesh['dp'=8,'mp'=4] {'mp'}, use_global_device_ids=true, to_apply=%region_27.0 | all-reduce | flops 3072 | bytes 24576 | tf_op jit(solution)/shard_map/psum | solution.py:40
  (41 shorter events, 25.4 us)
Async XLA Ops:
  6.5 35.9 %copy-start = (bf16[1024,256]{1,0:T(8,128)(2,1)S(1)}, bf16[1024,256]{1,0:T(8,128)(2,1)}, u32[]{:S(2)}) copy-start(bf16[1024,256]{1,0:T(8,128)(2,1)} %param.8) | copy-start | bytes 1572868
  6.5 132.2 %all-reduce.6.cloned.1.call-start = ((), (), s32[]{:S(2)}) async-start(), calls=%async_computation | async-start | bytes 2097152 | tf_op jit(solution)/shard_map/psum | solution.py:42
  42.5 3.8 copy-start.1
  42.5 15.1 %copy-start.5 = (f32[3072]{0:T(1024)S(1)}, f32[3072]{0:T(1024)}, u32[]{:S(2)}) copy-start(f32[3072]{0:T(1024)} %param.10) | copy-start | bytes 36868
  64.3 175.5 %all-reduce.8.cloned.1.call-start = ((), (), s32[]{:S(2)}) async-start(), calls=%async_computation.1 | async-start | bytes 2097152 | tf_op jit(solution)/shard_map/psum | solution.py:55
  155.2 84.7 %copy-start.2 = (f32[1024,256]{1,0:T(8,128)S(1)}, f32[1024,256]{1,0:T(8,128)}, u32[]{:S(2)}) copy-start(f32[1024,256]{1,0:T(8,128)} %all-reduce.6.cloned.1.call-done) | copy-start | bytes 3145732
  162.0 199.6 %all-reduce.10.cloned.1.call-start = ((), (), s32[]{:S(2)}) async-start(), calls=%async_computation.2 | async-start | bytes 2097152 | tf_op jit(solution)/shard_map/psum | solution.py:55
  260.2 2.2 copy-start.6
  284.5 199.2 %all-reduce.12.cloned.1.call-start = ((), (), s32[]{:S(2)}) async-start(), calls=%async_computation.3 | async-start | bytes 2097152 | tf_op jit(solution)/shard_map/psum | solution.py:55
  381.9 2.6 copy-start.7
  383.5 1.0 copy-start.4
  406.6 87.5 %copy-start.3 = (f32[1024,256]{1,0:T(8,128)S(1)}, f32[1024,256]{1,0:T(8,128)}, u32[]{:S(2)}) copy-start(f32[1024,256]{1,0:T(8,128)} %all-reduce.6.cloned.1.call-done) | copy-start | bytes 3145732
Sparse Core Ops, SparseCore 0:
  64.5 74.2 all-reduce.5
  162.1 77.7 all-reduce.7
  284.6 76.9 all-reduce.9
  406.8 76.9 all-reduce.11
where the time goes:
time: 519 us; the launch traced here: 518 us
  waiting for transfers between devices  306 us (59%)
  blocking collectives  116 us (22%)
  matrix products  56.2 us (11%)
  between operations  21 us (4%)
  other arithmetic  16.8 us (3%)
    psum x3, waiting for transfers between devices, shards(): lax.psum(pull_back(hidden_one, ((row_weight * tangent(spread(direction)))...  232 us
    psum x1, waiting for transfers between devices, shards(): gradient = lax.psum(pull_back(hidden_one, grad_back), 'dp')  74.4 us
    psum x4, blocking collectives, tangent(): return lax.psum(partial_rows, 'mp')  41.8 us
    psum x5, blocking collectives, inner_product(): return lax.psum(jnp.sum(first * second), 'mp')  33.7 us
    dot_general x4, matrix products, pull_back(): lax.dot_general(columns, back, (((0,), (0,)), ((), ())), preferred_elemen...  27 us
    psum x1, blocking collectives, shards(): valid_count = lax.psum(jnp.sum(valid_steps).astype(jnp.float32), 'dp')  23.6 us
    dot_general x4, matrix products, tangent(): jnp.dot(hidden_one, dir_bf16, preferred_element_type=jnp.float32)  22.8 us
    psum x1, blocking collectives, shards(): predicted = lax.psum(jnp.sum(hidden_two * out_weight, axis=-1), 'mp')  11.3 us
  transfers between devices with their start and end apart: 4, of which 4 were waited for; matrix products, arithmetic and copies ran while one was open for 0% of the time, Pallas kernels for 0%

commit v1 on v0

--- a/solution.py
+++ b/solution.py
@@ -39,7 +39,7 @@
         )
         return lax.psum(partial_rows, "mp")
 
-    gradient = lax.psum(pull_back(hidden_one, grad_back), "dp")
+    gradient = jnp.sum(lax.all_gather(pull_back(hidden_one, grad_back), "dp"), axis=0)
 
     def spread(vector):
         return vector.astype(jnp.bfloat16)

time: 519 us -> 569 us (1.096)
  waiting for transfers between devices: 306 us -> 351 us
    all_gather x0 -> x1, waiting for transfers between devices: none -> 121 us  [shards(): lax.all_gather(pull_back(hidden_one, grad_back), 'dp')]
    psum x1 -> x0, waiting for transfers between devices: 74.4 us -> none  [shards(): gradient = lax.psum(pull_back(hidden_one, grad_back), 'dp')]
where the time goes in v1:
time: 569 us; the launch traced here: 568 us
  waiting for transfers between devices  351 us (62%)
  blocking collectives  116 us (20%)
  matrix products  56.2 us (10%)
  between operations  21.2 us (4%)
  other arithmetic  20.8 us (4%)
    psum x3, waiting for transfers between devices, shards(): lax.psum(pull_back(hidden_one, ((row_weight * tangent(spread(direction)))...  230 us
    all_gather x1, waiting for transfers between devices, shards(): lax.all_gather(pull_back(hidden_one, grad_back), 'dp')  121 us
    psum x4, blocking collectives, tangent(): return lax.psum(partial_rows, 'mp')  42.5 us
    psum x5, blocking collectives, inner_product(): return lax.psum(jnp.sum(first * second), 'mp')  33.4 us
    dot_general x4, matrix products, pull_back(): lax.dot_general(columns, back, (((0,), (0,)), ((), ())), preferred_elemen...  26.9 us
    psum x1, blocking collectives, shards(): valid_count = lax.psum(jnp.sum(valid_steps).astype(jnp.float32), 'dp')  23.6 us
    dot_general x4, matrix products, tangent(): jnp.dot(hidden_one, dir_bf16, preferred_element_type=jnp.float32)  22.8 us
  transfers between devices with their start and end apart: 4, of which 4 were waited for; matrix products, arithmetic and copies ran while one was open for 0% of the time, Pallas kernels for 0%

profile of v1, /device:TPU:0, one launch (start us, length us, event | category | flops | bytes accessed | tf_op | source)
XLA Modules:
  0.0 567.8 jit_solution(7623745669956723177)
XLA Ops:
  8.5 23.6 %psum.105 = f32[]{:T(128)} all-reduce(f32[]{:T(128)S(6)} %convert_element_type.36), channel_id=1, replica_groups=mesh['dp'=8,'mp'=4] {'dp'}, use_global_device_ids=true, to_apply=%region_1.0 | all-reduce | flops 1 | bytes 8 | tf_op jit(solution)/shard_map/psum | solution.py:19
  34.3 5.4 all_gather.9
  46.2 11.3 %psum.106 = f32[3072]{0:T(1024)S(1)} all-reduce(f32[3072]{0:T(1024)S(1)} %get-tuple-element.11), channel_id=1, replica_groups=mesh['dp'=8,'mp'=4] {'mp'}, use_global_device_ids=true, to_apply=%region_3.0 | all-reduce | flops 3072 | bytes 24576 | tf_op jit(solution)/shard_map/psum | solution.py:26
  57.5 6.8 %fusion = f32[1024,256]{1,0:T(8,128)} fusion(bf16[3072,1024]{1,0:T(8,128)(2,1)} %copy-done.1, f32[3072]{0:T(1024)S(1)} %subtract_multiply_fusion.1, f32[3072,256]{0,1:T(8,128)} %get-tuple-element.12, f32[256]{0:T(256)S(1)} %convert_element_type.37), kind=kOutput, calls=%fused_computation.12 | convolution fusion | flops 1614544896 | bytes 10499072 | tf_op jit(solution)/shard_map/dot_general | solution.py:12
  64.4 121.3 %all-gather.3.cloned.1.call-done = f32[8192,256]{1,0:T(8,128)} async-done(((f32[1024,256]{1,0:T(8,128)}), f32[8192,256]{1,0:T(8,128)}) %all-gather.3.cloned.1.call-update) | async-done | bytes 8388624 | tf_op jit(solution)/shard_map/all_gather | solution.py:42
  189.8 6.3 %fusion.8 = f32[3072]{0:T(1024)S(1)} fusion(bf16[3072,1024]{1,0:T(8,128)(2,1)} %copy-done.1, f32[1024,256]{1,0:T(8,128)S(1)} %reduce_sum.119, f32[256]{0:T(256)S(1)} %convert_element_type.37, f32[3072,256]{0,1:T(8,128)} %get-tuple-element.12), kind=kOutput, calls=%fused_computation.20 | convolution fusion | flops 1615066112 | bytes 10499072 | tf_op jit(solution)/shard_map/dot_general | solution.py:38
  196.1 10.4 %psum.108 = f32[3072]{0:T(1024)S(1)} all-reduce(f32[3072]{0:T(1024)S(1)} %fusion.8), channel_id=1, replica_groups=mesh['dp'=8,'mp'=4] {'mp'}, use_global_device_ids=true, to_apply=%region_8.0 | all-reduce | flops 3072 | bytes 24576 | tf_op jit(solution)/shard_map/psum | solution.py:40
  206.5 6.7 %fusion.1 = f32[1024,256]{1,0:T(8,128)} fusion(bf16[3072,1024]{1,0:T(8,128)(2,1)} %copy-done.1, f32[3072]{0:T(1024)S(1)} %mul.147, f32[3072,256]{0,1:T(8,128)} %get-tuple-element.12, f32[256]{0:T(256)S(1)} %convert_element_type.37), kind=kOutput, calls=%fused_computation.13 | convolution fusion | flops 1614544896 | bytes 10499072 | tf_op jit(solution)/shard_map/dot_general | solution.py:12
  213.3 76.1 %all-reduce.5.cloned.1.call-done = f32[1024,256]{1,0:T(8,128)} async-done(((f32[1024,256]{1,0:T(8,128)}), f32[1024,256]{1,0:T(8,128)}) %all-reduce.5.cloned.1.call-update) | async-done | bytes 1048592 | tf_op jit(solution)/shard_map/psum | solution.py:55
  291.6 6.5 %all-reduce = (f32[]{:T(128)}, f32[]{:T(128)}) all-reduce(f32[]{:T(128)} %get-tuple-element.6, f32[]{:T(128)} %get-tuple-element.5), channel_id=1, replica_groups=mesh['dp'=8,'mp'=4] {'mp'}, use_global_device_ids=true, to_apply=%region_6.0 | all-reduce | flops 2 | bytes 16 | tf_op jit(solution)/shard_map/psum | solution.py:48
  301.5 7.0 %psum.111 = f32[]{:T(128)} all-reduce(f32[]{:T(128)} %get-tuple-element.9), channel_id=1, replica_groups=mesh['dp'=8,'mp'=4] {'mp'}, use_global_device_ids=true, to_apply=%region_13.0 | all-reduce | flops 1 | bytes 8 | tf_op jit(solution)/shard_map/psum | solution.py:48
  312.0 5.1 fusion.9
  317.1 10.2 %psum.112 = f32[3072]{0:T(1024)S(1)} all-reduce(f32[3072]{0:T(1024)S(1)} %fusion.9), channel_id=1, replica_groups=mesh['dp'=8,'mp'=4] {'mp'}, use_global_device_ids=true, to_apply=%region_15.0 | all-reduce | flops 3072 | bytes 24576 | tf_op jit(solution)/shard_map/psum | solution.py:40
  327.3 6.7 %fusion.2 = f32[1024,256]{1,0:T(8,128)} fusion(bf16[3072,1024]{1,0:T(8,128)(2,1)} %copy-done.1, f32[3072]{0:T(1024)S(1)} %mul.159, f32[3072,256]{0,1:T(8,128)} %get-tuple-element.12, f32[256]{0:T(256)S(1)} %convert_element_type.37), kind=kOutput, calls=%fused_computation.14 | convolution fusion | flops 1614544896 | bytes 10499072 | tf_op jit(solution)/shard_map/dot_general | solution.py:12
  334.1 77.1 %all-reduce.7.cloned.1.call-done = f32[1024,256]{1,0:T(8,128)} async-done(((f32[1024,256]{1,0:T(8,128)}), f32[1024,256]{1,0:T(8,128)}) %all-reduce.7.cloned.1.call-update) | async-done | bytes 1048592 | tf_op jit(solution)/shard_map/psum | solution.py:55
  413.3 6.5 %psum.114 = f32[]{:T(128)} all-reduce(f32[]{:T(128)} %multiply_reduce_fusion.3), channel_id=1, replica_groups=mesh['dp'=8,'mp'=4] {'mp'}, use_global_device_ids=true, to_apply=%region_18.0 | all-reduce | flops 1 | bytes 8 | tf_op jit(solution)/shard_map/psum | solution.py:48
  423.2 7.0 %psum.115 = f32[]{:T(128)} all-reduce(f32[]{:T(128)} %multiply_reduce_fusion.2), channel_id=1, replica_groups=mesh['dp'=8,'mp'=4] {'mp'}, use_global_device_ids=true, to_apply=%region_20.0 | all-reduce | flops 1 | bytes 8 | tf_op jit(solution)/shard_map/psum | solution.py:48
  434.1 5.2 fusion.10
  439.3 10.7 %psum.116 = f32[3072]{0:T(1024)S(1)} all-reduce(f32[3072]{0:T(1024)S(1)} %fusion.10), channel_id=1, replica_groups=mesh['dp'=8,'mp'=4] {'mp'}, use_global_device_ids=true, to_apply=%region_22.0 | all-reduce | flops 3072 | bytes 24576 | tf_op jit(solution)/shard_map/psum | solution.py:40
  450.0 6.7 %fusion.3 = f32[1024,256]{1,0:T(8,128)} fusion(bf16[3072,1024]{1,0:T(8,128)(2,1)} %copy-done.1, f32[3072]{0:T(1024)S(1)} %mul.171, f32[3072,256]{0,1:T(8,128)} %get-tuple-element.12, f32[256]{0:T(256)S(1)} %convert_element_type.37), kind=kOutput, calls=%fused_computation.15 | convolution fusion | flops 1614544896 | bytes 10499072 | tf_op jit(solution)/shard_map/dot_general | solution.py:12
  456.7 76.9 %all-reduce.9.cloned.1.call-done = f32[1024,256]{1,0:T(8,128)} async-done(((f32[1024,256]{1,0:T(8,128)}), f32[1024,256]{1,0:T(8,128)}) %all-reduce.9.cloned.1.call-update) | async-done | bytes 1048592 | tf_op jit(solution)/shard_map/psum | solution.py:55
  536.0 6.5 %psum.118 = f32[]{:T(128)} all-reduce(f32[]{:T(128)} %multiply_reduce_fusion.1), channel_id=1, replica_groups=mesh['dp'=8,'mp'=4] {'mp'}, use_global_device_ids=true, to_apply=%region_25.0 | all-reduce | flops 1 | bytes 8 | tf_op jit(solution)/shard_map/psum | solution.py:48
  543.8 6.3 %fusion.11 = f32[3072]{0:T(1024)S(1)} fusion(bf16[3072,1024]{1,0:T(8,128)(2,1)} %copy-done.1, f32[1024,256]{1,0:T(8,128)} %copy-done.4, f32[1024,256]{1,0:T(8,128)S(1)} %multiply_add_fusion.2, f32[1024,256]{1,0:T(8,128)S(1)} %copy-done.3, f32[]{:T(128)S(6)} %div.30, f32[]{:T(128)S(6)} %div.28, f32[]{:T(128)S(6)} %div.26, f32[256]{0:T(256)S(1)} %convert_element_type.37, ...), kind=kOutput, calls=%fused_computation.23 | convolution fusion | flops 1616376832 | bytes 12596236 | tf_op jit(solution)/shard_map/dot_general | solution.py:38
  550.0 11.2 %psum.119 = f32[3072]{0:T(1024)} all-reduce(f32[3072]{0:T(1024)S(1)} %fusion.11), channel_id=1, replica_groups=mesh['dp'=8,'mp'=4] {'mp'}, use_global_device_ids=true, to_apply=%region_27.0 | all-reduce | flops 3072 | bytes 24576 | tf_op jit(solution)/shard_map/psum | solution.py:40
  (42 shorter events, 29.2 us)
Async XLA Ops:
  6.5 35.9 %copy-start = (bf16[1024,256]{1,0:T(8,128)(2,1)S(1)}, bf16[1024,256]{1,0:T(8,128)(2,1)}, u32[]{:S(2)}) copy-start(bf16[1024,256]{1,0:T(8,128)(2,1)} %param.8) | copy-start | bytes 1572868
  6.5 179.2 %all-gather.3.cloned.1.call-start = ((), (), s32[]{:S(2)}) async-start(), calls=%async_computation.3 | async-start | bytes 9437184 | tf_op jit(solution)/shard_map/all_gather | solution.py:42
  42.5 3.7 copy-start.1
  42.5 15.0 %copy-start.5 = (f32[3072]{0:T(1024)S(1)}, f32[3072]{0:T(1024)}, u32[]{:S(2)}) copy-start(f32[3072]{0:T(1024)} %param.10) | copy-start | bytes 36868
  64.3 225.1 %all-reduce.5.cloned.1.call-start = ((), (), s32[]{:S(2)}) async-start(), calls=%async_computation | async-start | bytes 2097152 | tf_op jit(solution)/shard_map/psum | solution.py:55
  189.8 109.6 %copy-start.2 = (f32[1024,256]{1,0:T(8,128)}, f32[1024,256]{1,0:T(8,128)S(1)}, u32[]{:S(2)}) copy-start(f32[1024,256]{1,0:T(8,128)S(1)} %reduce_sum.119) | copy-start | bytes 3145732
  213.3 197.9 %all-reduce.7.cloned.1.call-start = ((), (), s32[]{:S(2)}) async-start(), calls=%async_computation.1 | async-start | bytes 2097152 | tf_op jit(solution)/shard_map/psum | solution.py:55
  309.8 2.2 copy-start.6
  334.1 199.5 %all-reduce.9.cloned.1.call-start = ((), (), s32[]{:S(2)}) async-start(), calls=%async_computation.2 | async-start | bytes 2097152 | tf_op jit(solution)/shard_map/psum | solution.py:55
  431.5 2.6 copy-start.7
  433.1 1.0 copy-start.4
  456.7 87.1 %copy-start.3 = (f32[1024,256]{1,0:T(8,128)S(1)}, f32[1024,256]{1,0:T(8,128)}, u32[]{:S(2)}) copy-start(f32[1024,256]{1,0:T(8,128)} %copy-done.2) | copy-start | bytes 3145732
Sparse Core Ops, SparseCore 0:
  64.4 121.2 all-gather.2
  213.4 75.9 all-reduce.4
  334.2 76.9 all-reduce.6
  456.8 76.6 all-reduce.8
